TPU v7x, 128 devices: a whole 4x4x4 slice. The times are simulated.
128 devices in a mesh: sub: 2 (over z_hi), vox: 64 (over y, x, z_lo, core).
Axes of the slice: x: 4, y: 4, z: 4 (z_hi: 2, z_lo: 2; z = z_hi * 2 + z_lo), core: 2. Of those that a mesh axis runs over, the one named last changes fastest.
Arguments:
- observed: float32 [2048, 131072], P('sub', 'vox'), may hold values from -6 to 6
- covariates: float32 [2048, 64], P('sub'), may hold values from -0.26516504 to 0.26516504
- voxel_mask: int32 [131072], P('vox'), may hold values 0 or 1
- tau_index: int32 [1], replicated, may hold values from 2 to 18
Outputs:
- coefficients: float32 [64, 131072], P(None, 'vox')
- split_residual: float32 [2048, 131072], P('sub', 'vox')
All inputs are finite; a program needn't handle non-finite values. Where the computation divides by a largest or mean magnitude, that divisor is 1e-20 or more. No bound on the sum of `voxel_mask` on one device may be relied on, other than what follows from the above.
Results may differ from a plain program's by a relative error of at most 0.0001.
Values sent between devices are 32-bit elements; how exact they have to be, the bound alone decides.
A program may use at most 128 MiB of HBM per device.

v0:
```python
import functools

import jax
import jax.numpy as jnp
from jax import lax
from jax.experimental import pallas as pl
from jax.experimental.pallas import tpu as pltpu
from jax.sharding import PartitionSpec as P

COVARS = 64
PX = 8
PY = 8
GZ = 32
NPY = 8
QUANT = 20
LAYER = PY * GZ
ROWS = 256

penalty_fit = 1.0
penalty_tv = 1.0
tv_weight = 0.05
huber_width = 0.02
BOUND = tv_weight / penalty_tv
RATIO = BOUND / (huber_width + BOUND)

MESH = pl.DeviceIdType.MESH
F32 = jnp.float32
BF16 = jnp.bfloat16


def halves(value):
    high = value.astype(BF16)
    return high, (value - high.astype(F32)).astype(BF16)


def product(left, right):
    return jnp.dot(left, right, preferred_element_type=F32)


def stacked(coef):
    high, low = halves(coef)
    return jnp.concatenate([high, high, low, low], 0)


def dual_of(target):
    return jnp.clip(target * RATIO, -BOUND, BOUND)


def levels(tau_ref):
    quantile = tau_ref[0].astype(F32) / QUANT
    return (quantile - 1.0) / penalty_fit, quantile / penalty_fit


def iterate(
    image_hbm, covs_ref, mask_ref, tau_ref,
    base_out, coef_out, split_out,
    image, dual, sums, partner, coefs, first_v, w_x, w_y, w_z, w_edge,
    edge_out, edge_in, gram_out, gram_in, covs_t,
    load_sem, sum_send, sum_recv, x_send, x_recv, y_send, y_recv, gram_send, gram_recv,
):
    part = lax.axis_index("sub")
    place = lax.axis_index("vox")
    pencils = lax.axis_size("vox")
    mate = (1 - part, place)
    right_x = (part, lax.rem(place + NPY, pencils))
    left_x = (part, lax.rem(place + pencils - NPY, pencils))
    right_y = (part, lax.rem(place + 1, pencils))
    left_y = (part, lax.rem(place + pencils - 1, pencils))
    pencil_y = lax.rem(lax.rem(place + NPY // 2, pencils), NPY)

    barrier = pltpu.get_barrier_semaphore()
    for device in (mate, right_x, left_x, right_y, left_y):
        pl.semaphore_signal(barrier, inc=1, device_id=device, device_id_type=MESH)

    def load(x):
        return pltpu.make_async_copy(
            image_hbm.at[:, pl.ds(pl.multiple_of(x * LAYER, LAYER), LAYER)],
            image.at[x], load_sem.at[x],
        )

    def send_sum(step, x):
        return pltpu.make_async_remote_copy(
            src_ref=sums.at[step, x], dst_ref=partner.at[step, x],
            send_sem=sum_send.at[step, x], recv_sem=sum_recv.at[step, x],
            device_id=mate, device_id_type=MESH,
        )

    def send_x(step, way):
        source, target, device = ((1, PX + 1, left_x), (PX, 0, right_x))[way]
        return pltpu.make_async_remote_copy(
            src_ref=coefs.at[step, source], dst_ref=coefs.at[step, target],
            send_sem=x_send.at[step, way], recv_sem=x_recv.at[step, way],
            device_id=device, device_id_type=MESH,
        )

    def send_y(step, way, half):
        return pltpu.make_async_remote_copy(
            src_ref=edge_out.at[step, way, half], dst_ref=edge_in.at[step, way, half],
            send_sem=y_send.at[step, way, half], recv_sem=y_recv.at[step, way, half],
            device_id=(left_y, right_y)[way], device_id_type=MESH,
        )

    send_gram = pltpu.make_async_remote_copy(
        src_ref=gram_out, dst_ref=gram_in, send_sem=gram_send, recv_sem=gram_recv,
        device_id=mate, device_id_type=MESH,
    )

    for x in range(PX):
        load(x).start()

    turned = covs_ref[...]
    high, low = halves(turned)
    covs_t[...] = jnp.concatenate([high, low], 0)
    pair = jnp.concatenate([high.astype(F32), low.astype(F32)], 0).T.astype(BF16)
    split_out[...] = jnp.concatenate([pair, pair], 1)
    gram_out[...] = lax.dot_general(
        turned, turned, (((1,), (1,)), ((), ())),
        precision=lax.Precision.HIGHEST, preferred_element_type=F32,
    )
    edge_out[...] = jnp.zeros_like(edge_out)

    floor, ceiling = levels(tau_ref)
    lane = lax.broadcasted_iota(jnp.int32, (COVARS, LAYER), 1)
    short = lax.broadcasted_iota(jnp.int32, (COVARS, 128), 1)
    valid_y = ((lane < LAYER - GZ) | (pencil_y < NPY - 1)).astype(F32)
    valid_z = (lax.rem(lane, GZ) < GZ - 1).astype(F32)
    has_left = ((short < GZ) & (pencil_y > 0)).astype(F32)

    def mask_of(x):
        return mask_ref[:, pl.ds(pl.multiple_of(x * LAYER, LAYER), LAYER)].astype(F32)

    def add_up(total, rows, high, low):
        both = product(covs_t[:, rows], high)
        one = product(covs_t[0:COVARS, rows], low)
        term = both[0:COVARS] + both[COVARS:] + one
        return term if total is None else total + term

    def first(x, carry):
        load(x).wait()
        total = None
        for block in range(image.shape[1] // ROWS):
            rows = slice(block * ROWS, (block + 1) * ROWS)
            total = add_up(total, rows, *halves(image[x, rows, :]))
        sums[0, x] = total * mask_of(x)
        send_sum(0, x).start()
        return carry

    pl.semaphore_wait(barrier, 5)
    send_gram.start()
    lax.fori_loop(0, PX, first, 0)

    send_gram.wait()
    gram = gram_out[...] + gram_in[...]
    row_bound = jnp.max(jnp.sum(jnp.abs(gram), axis=1, keepdims=True), axis=0, keepdims=True)
    eta = 1.0 / (penalty_fit * row_bound + 12.0 * penalty_tv)

    def pass_on(step, x, coef):
        coefs[step, x + 1] = coef
        quarter = lax.rem(x, 4)
        half = lax.div(x, 4)
        here = lax.div(short, GZ) == quarter
        front = pltpu.roll(coef[:, 0:128], quarter * GZ, 1)
        back = pltpu.roll(coef[:, 128:256], lax.rem(quarter * GZ + GZ, 128), 1)
        edge_out[step, 0, half] = jnp.where(here, front, edge_out[step, 0, half])
        edge_out[step, 1, half] = jnp.where(here, back, edge_out[step, 1, half])

        @pl.when(x == 0)
        def _():
            send_x(step, 0).start()

        @pl.when(x == PX - 1)
        def _():
            send_x(step, 1).start()

        for part_of in range(2):
            @pl.when(x == 4 * part_of + 3)
            def _():
                send_y(step, 0, part_of).start()
                send_y(step, 1, part_of).start()

    def residual(step, x, coef):
        right = stacked(coef)
        total = None
        for block in range(image.shape[1] // ROWS):
            rows = slice(block * ROWS, (block + 1) * ROWS)
            seen = image[x, rows, :]
            target = seen - product(split_out[rows, :], right)
            if step == 1:
                target = target + dual[x, rows, :]
            new = jnp.clip(target, floor, ceiling)
            if step == 0:
                dual[x, rows, :] = new
            else:
                base_out[x, rows, :] = seen + new
            total = add_up(total, rows, *halves(new))
        sums[step + 1, x] = total * mask_of(x)
        send_sum(step + 1, x).start()

    def smooth(step, x):
        for part_of in range(2):
            @pl.when(x == 4 * part_of)
            def _():
                send_y(step, 0, part_of).wait_recv()
                send_y(step, 1, part_of).wait_recv()

        @pl.when(x == 0)
        def _():
            send_x(step, 1).wait_recv()
            rise = coefs[step, 1] - coefs[step, 0]
            if step == 1:
                rise = rise + w_x[0]
            w_x[0] = dual_of(rise)

        @pl.when(x == PX - 1)
        def _():
            send_x(step, 0).wait_recv()

        quarter = lax.rem(x, 4)
        half = lax.div(x, 4)
        here = coefs[step, x + 1]
        rise_x = coefs[step, x + 2] - here
        after = pltpu.roll(edge_in[step, 0, half], (128 - GZ) - quarter * GZ, 1)
        before = pltpu.roll(edge_in[step, 1, half], lax.rem(128 - quarter * GZ, 128), 1)
        turned_y = pltpu.roll(here, LAYER - GZ, 1)
        next_y = jnp.concatenate(
            [turned_y[:, 0:128], jnp.where(short >= 128 - GZ, after, turned_y[:, 128:256])], 1
        )
        rise_y = valid_y * (next_y - here)
        rise_z = valid_z * (pltpu.roll(here, LAYER - 1, 1) - here)
        rise_edge = has_left * (here[:, 0:128] - before)
        if step == 1:
            rise_x = rise_x + w_x[x + 1]
            rise_y = rise_y + w_y[x]
            rise_z = rise_z + w_z[x]
            rise_edge = rise_edge + w_edge[x]
        new_x, new_y, new_z, new_edge = (dual_of(rise) for rise in (rise_x, rise_y, rise_z, rise_edge))
        summed = w_x[x] - new_x
        turned_y = pltpu.roll(new_y, GZ, 1)
        prev_y = jnp.concatenate(
            [jnp.where(short < GZ, new_edge, turned_y[:, 0:128]), turned_y[:, 128:256]], 1
        )
        summed = summed + (prev_y - new_y)
        summed = summed + (pltpu.roll(new_z, 1, 1) - new_z)
        w_x[x + 1] = new_x
        if step == 0:
            w_y[x] = new_y
            w_z[x] = new_z
            w_edge[x] = new_edge
        return summed

    def second(x, carry):
        send_sum(0, x).wait_recv()
        coef = eta * (sums[0, x] + partner[0, x])
        pass_on(0, x, coef)
        residual(0, x, coef)
        return carry

    def third(x, carry):
        summed = smooth(0, x)
        send_sum(1, x).wait_recv()
        change = (sums[1, x] + partner[1, x]) - summed
        first_v[x] = change
        coef = coefs[0, x + 1] + eta * (2.0 * change)
        pass_on(1, x, coef)
        residual(1, x, coef)
        return carry

    def last(x, carry):
        summed = smooth(1, x)
        send_sum(2, x).wait_recv()
        change = (sums[2, x] + partner[2, x]) - summed
        coef_out[x] = coefs[1, x + 1] + eta * (2.0 * change - first_v[x])
        return carry

    lax.fori_loop(0, PX, second, 0)
    lax.fori_loop(0, PX, third, 0)
    lax.fori_loop(0, PX, last, 0)

    for step in range(3):
        for x in range(PX):
            send_sum(step, x).wait_send()
    for step in range(2):
        for way in range(2):
            send_x(step, way).wait_send()
            for half in range(2):
                send_y(step, way, half).wait_send()


def finish(base, coef_ref, split_ref, mask_ref, tau_ref, coef_out, residual_out, result, out_sem, coef_sem):
    floor, ceiling = levels(tau_ref)

    def columns(x):
        return pl.ds(pl.multiple_of(x * LAYER, LAYER), LAYER)

    def put(x):
        return pltpu.make_async_copy(result.at[x], residual_out.at[:, columns(x)], out_sem.at[x])

    def put_coef(x):
        return pltpu.make_async_copy(coef_ref.at[x], coef_out.at[:, columns(x)], coef_sem.at[x])

    for x in range(PX):
        put_coef(x).start()

    def layer(x, carry):
        right = stacked(coef_ref[x])
        mask = mask_ref[:, columns(x)].astype(F32)
        for block in range(result.shape[1] // ROWS):
            rows = slice(block * ROWS, (block + 1) * ROWS)
            target = base[x, rows, :] - product(split_ref[rows, :], right)
            result[x, rows, :] = mask * (target - jnp.clip(target, floor, ceiling))
        put(x).start()
        return carry

    lax.fori_loop(0, PX, layer, 0)
    for x in range(PX):
        put_coef(x).wait()
        put(x).wait()


def per_device(observed, covariates, voxel_mask, tau_index):
    subjects, voxels = observed.shape
    mask = voxel_mask.reshape(1, voxels)
    vmem = pl.BlockSpec(memory_space=pltpu.VMEM)
    smem = pl.BlockSpec(memory_space=pltpu.SMEM)
    hbm = pl.BlockSpec(memory_space=pl.ANY)
    dma = pltpu.SemaphoreType.DMA
    base, coef, split = pl.pallas_call(
        iterate,
        out_shape=(
            pltpu.VMEM((PX, subjects, LAYER), F32),
            pltpu.VMEM((PX, COVARS, LAYER), F32),
            pltpu.VMEM((subjects, 4 * COVARS), BF16),
        ),
        in_specs=[hbm, vmem, vmem, smem],
        out_specs=(vmem, vmem, vmem),
        scratch_shapes=[
            pltpu.VMEM((PX, subjects, LAYER), F32),
            pltpu.VMEM((PX, subjects, LAYER), F32),
            pltpu.VMEM((3, PX, COVARS, LAYER), F32),
            pltpu.VMEM((3, PX, COVARS, LAYER), F32),
            pltpu.VMEM((2, PX + 2, COVARS, LAYER), F32),
            pltpu.VMEM((PX, COVARS, LAYER), F32),
            pltpu.VMEM((PX + 1, COVARS, LAYER), F32),
            pltpu.VMEM((PX, COVARS, LAYER), F32),
            pltpu.VMEM((PX, COVARS, LAYER), F32),
            pltpu.VMEM((PX, COVARS, 128), F32),
            pltpu.VMEM((2, 2, 2, COVARS, 128), F32),
            pltpu.VMEM((2, 2, 2, COVARS, 128), F32),
            pltpu.VMEM((COVARS, COVARS), F32),
            pltpu.VMEM((COVARS, COVARS), F32),
            pltpu.VMEM((2 * COVARS, subjects), BF16),
            dma((PX,)), dma((3, PX)), dma((3, PX)), dma((2, 2)), dma((2, 2)),
            dma((2, 2, 2)), dma((2, 2, 2)), dma, dma,
        ],
        compiler_params=pltpu.CompilerParams(
            collective_id=0, has_side_effects=True, vmem_limit_bytes=40 << 20
        ),
        name="iterate",
    )(observed, covariates.T, mask, tau_index)
    return pl.pallas_call(
        finish,
        out_shape=(
            jax.ShapeDtypeStruct((COVARS, voxels), F32),
            jax.ShapeDtypeStruct((subjects, voxels), F32),
        ),
        in_specs=[vmem, vmem, vmem, vmem, smem],
        out_specs=(hbm, hbm),
        scratch_shapes=[pltpu.VMEM((PX, subjects, LAYER), F32), dma((PX,)), dma((PX,))],
        compiler_params=pltpu.CompilerParams(vmem_limit_bytes=24 << 20),
        name="finish",
    )(base, coef, split, mask, tau_index)


def solution(mesh):
    return jax.shard_map(
        per_device,
        mesh=mesh,
        in_specs=(P("sub", "vox"), P("sub", None), P("vox"), P()),
        out_specs=(P(None, "vox"), P("sub", "vox")),
        check_vma=False,
    )
```

profile of v0, /device:TPU:1, one launch (start us, length us, event | category | flops | bytes accessed | tf_op | source)
XLA Modules:
  0.0 55.8 jit_solution(15580127899195369543)
XLA Ops:
  1.3 0.0 copy-start
  1.3 0.9 %copy-done = f32[1024,64]{0,1:T(8,128)S(1)} copy-done((f32[1024,64]{0,1:T(8,128)S(1)}, f32[1024,64]{0,1:T(8,128)}, u32[]{:S(2)}) %copy-start) | copy-done | bytes 262168
  2.2 0.0 copy-start.1
  2.2 0.7 %copy-done.1 = s32[2048]{0:T(1024)S(1)} copy-done((s32[2048]{0:T(1024)S(1)}, s32[2048]{0:T(1024)}, u32[]{:S(2)}) %copy-start.1) | copy-done | bytes 8216
  2.9 48.9 %iterate.1 = (f32[8,1024,256]{2,1,0:T(8,128)S(1)}, f32[8,64,256]{2,1,0:T(8,128)S(1)}, bf16[1024,256]{1,0:T(8,128)(2,1)S(1)}) custom-call(f32[1024,2048]{1,0:T(8,128)} %image_hbm.1, f32[64,1024]{1,0:T(8,128)S(1)} %bitcast.2, s32[1,2048]{1,0:T(1,128)S(1)} %bitcast.3, s32[1]{0:T(128)S(6)} %copy.6.tau_ref), custom_call_target="tpu_custom_call" | custom-call | tf_op jit(solution)/shard_map/iterate/pallas_call | solution.py:327
  51.8 4.0 %finish.1 = (f32[64,2048]{1,0:T(8,128)}, f32[1024,2048]{1,0:T(8,128)}) custom-call(f32[8,1024,256]{2,1,0:T(8,128)S(1)} %get-tuple-element.5.base, f32[8,64,256]{2,1,0:T(8,128)S(1)} %get-tuple-element.6.coef_ref, bf16[1024,256]{1,0:T(8,128)(2,1)S(1)} %get-tuple-element.7.split_ref, s32[1,2048]{1,0:T(1,128)S(1)} %bitcast.4, s32[1]{0:T(128)S(6)} %copy.6.tau_ref), custom_call_target="tpu_custom_call" | custom-call | tf_op jit(solution)/shard_map/finish/pallas_call | solution.py:360
Async XLA Ops:
  1.3 1.0 %copy-start = (f32[1024,64]{0,1:T(8,128)S(1)}, f32[1024,64]{0,1:T(8,128)}, u32[]{:S(2)}) copy-start(f32[1024,64]{0,1:T(8,128)} %param.5) | copy-start | bytes 786436
  2.2 0.7 %copy-start.1 = (s32[2048]{0:T(1024)S(1)}, s32[2048]{0:T(1024)}, u32[]{:S(2)}) copy-start(s32[2048]{0:T(1024)} %param.6) | copy-start | bytes 24580
where the time goes:
time: 56 us; the launch traced here: 55.8 us
  Pallas kernels  52.9 us (94%)
  local copies, waits for them, and re-layouts  1.64 us (3%)
  between operations  1.29 us (2%)
    pallas_call x1, Pallas kernels, per_device(): pl.pallas_call(iterate, out_shape=(pltpu.VMEM((PX, subjects, LAYER), F32)...  48.9 us
    pallas_call x1, Pallas kernels, per_device(): pl.pallas_call(finish, out_shape=(jax.ShapeDtypeStruct((COVARS, voxels),...  4.01 us
    unnamed x4, local copies, waits for them, and re-layouts  1.64 us

commit v1 on v0

v1 whole, which is shorter than its diff:
```python
import functools

import jax
import jax.numpy as jnp
from jax import lax
from jax.experimental import pallas as pl
from jax.experimental.pallas import tpu as pltpu
from jax.sharding import PartitionSpec as P

COVARS = 64
PX = 8
PY = 8
GZ = 32
NPY = 8
QUANT = 20
LAYER = PY * GZ
ROWS = 256
WINDOW = 2

penalty_fit = 1.0
penalty_tv = 1.0
tv_weight = 0.05
huber_width = 0.02
BOUND = tv_weight / penalty_tv
RATIO = BOUND / (huber_width + BOUND)

MESH = pl.DeviceIdType.MESH
F32 = jnp.float32
BF16 = jnp.bfloat16


def halves(value):
    high = value.astype(BF16)
    return high, (value - high.astype(F32)).astype(BF16)


def product(left, right):
    return jnp.dot(left, right, preferred_element_type=F32)


def stacked(coef):
    high, low = halves(coef)
    return jnp.concatenate([high, high, low, low], 0)


def dual_of(target):
    return jnp.clip(target * RATIO, -BOUND, BOUND)


def levels(tau_ref):
    quantile = tau_ref[0].astype(F32) / QUANT
    return (quantile - 1.0) / penalty_fit, quantile / penalty_fit


def iterate(
    image_hbm, covs_hbm, mask_hbm, tau_ref,
    base_out, coef_out, split_out, mask_out, level_out,
    image, dual, sums, partner, coefs, first_v, w_x, w_y, w_z, w_edge,
    edge_out, edge_in, gram_out, gram_in, covs_t, covs_ref, mask_ref,
    load_sem, covs_sem, mask_sem, sum_send, sum_recv, x_send, x_recv, y_send, y_recv, gram_send, gram_recv,
):
    part = lax.axis_index("sub")
    place = lax.axis_index("vox")
    pencils = lax.axis_size("vox")
    mate = (1 - part, place)
    right_x = (part, lax.rem(place + NPY, pencils))
    left_x = (part, lax.rem(place + pencils - NPY, pencils))
    right_y = (part, lax.rem(place + 1, pencils))
    left_y = (part, lax.rem(place + pencils - 1, pencils))
    crosses = lax.rem(place, 2)
    far_y = (lax.rem(part + crosses, 2), right_y[1])
    behind_y = (lax.rem(part + 1 - crosses, 2), left_y[1])
    pencil_y = lax.rem(lax.rem(place + NPY // 2, pencils), NPY)

    barrier = pltpu.get_barrier_semaphore()
    for device in (mate, right_x, left_x, right_y, behind_y):
        pl.semaphore_signal(barrier, inc=1, device_id=device, device_id_type=MESH)

    def layer_at(turn):
        return lax.rem(turn + PX - 1, PX)

    def load(x):
        return pltpu.make_async_copy(
            image_hbm.at[:, pl.ds(pl.multiple_of(x * LAYER, LAYER), LAYER)],
            image.at[x], load_sem.at[x],
        )

    def send_sum(number):
        return pltpu.make_async_remote_copy(
            src_ref=sums.at[number], dst_ref=partner.at[number],
            send_sem=sum_send.at[number], recv_sem=sum_recv.at[number],
            device_id=mate, device_id_type=MESH,
        )

    def give_sum(number):
        @pl.when(number >= WINDOW)
        def _():
            send_sum(number - WINDOW).wait_send()

        send_sum(number).start()

    def send_x(step, way):
        source, target, device = ((1, PX + 1, left_x), (PX, 0, right_x))[way]
        return pltpu.make_async_remote_copy(
            src_ref=coefs.at[step, source], dst_ref=coefs.at[step, target],
            send_sem=x_send.at[step, way], recv_sem=x_recv.at[step, way],
            device_id=device, device_id_type=MESH,
        )

    def send_y(step, way, x):
        return pltpu.make_async_remote_copy(
            src_ref=edge_out.at[step, way, x], dst_ref=edge_in.at[step, way, x],
            send_sem=y_send.at[step, way, x], recv_sem=y_recv.at[step, way, x],
            device_id=(left_y, far_y)[way], device_id_type=MESH,
        )

    send_gram = pltpu.make_async_remote_copy(
        src_ref=gram_out, dst_ref=gram_in, send_sem=gram_send, recv_sem=gram_recv,
        device_id=mate, device_id_type=MESH,
    )

    load_covs = pltpu.make_async_copy(covs_hbm, covs_ref, covs_sem)
    load_mask = pltpu.make_async_copy(mask_hbm, mask_ref, mask_sem)
    load_covs.start()
    load_mask.start()
    for turn in range(2):
        load(layer_at(turn)).start()

    load_covs.wait()
    covs = covs_ref[...]
    high, low = halves(covs)
    covs_t[...] = jnp.concatenate([high, low], 0)
    load_mask.wait()
    mask_out[...] = mask_ref[...].astype(F32)

    lane = lax.broadcasted_iota(jnp.int32, (COVARS, LAYER), 1)
    short = lax.broadcasted_iota(jnp.int32, (COVARS, 128), 1)
    valid_y = ((lane < LAYER - GZ) | (pencil_y < NPY - 1)).astype(F32)
    valid_z = (lax.rem(lane, GZ) < GZ - 1).astype(F32)
    has_left = ((short < GZ) & (pencil_y > 0)).astype(F32)

    def mask_of(x):
        return mask_out[:, pl.ds(pl.multiple_of(x * LAYER, LAYER), LAYER)]

    def packed(block):
        rows = COVARS // 4
        result = block[0:rows]
        for group in range(1, 4):
            moved = pltpu.roll(block[group * rows : (group + 1) * rows], group * GZ, 1)
            result = jnp.where(lax.div(short[0:rows], GZ) == group, moved, result)
        return result

    def unpacked(block, lane_at):
        moved = [(lane_at - group * GZ) % 128 for group in range(4)]
        return jnp.concatenate([pltpu.roll(block, by, 1) if by else block for by in moved], 0)

    def add_up(total, rows, high, low):
        both = product(covs_t[:, rows], high)
        one = product(covs_t[0:COVARS, rows], low)
        term = both[0:COVARS] + both[COVARS:] + one
        return term if total is None else total + term

    def first(turn, carry):
        x = layer_at(turn)
        load(x).wait()

        @pl.when(turn + 2 < PX)
        def _():
            load(layer_at(turn + 2)).start()

        total = None
        for block in range(image.shape[1] // ROWS):
            rows = slice(block * ROWS, (block + 1) * ROWS)
            total = add_up(total, rows, *halves(image[x, rows, :]))
        sums[turn] = total * mask_of(x)

        @pl.when(turn == 0)
        def _():
            pl.semaphore_wait(barrier, 5)

        give_sum(turn)

        @pl.when(turn == 0)
        def _():
            gram_out[...] = lax.dot_general(
                covs, covs, (((1,), (1,)), ((), ())),
                precision=lax.Precision.HIGHEST, preferred_element_type=F32,
            )
            send_gram.start()

        return carry

    lax.fori_loop(0, PX, first, 0)
    pair = jnp.concatenate([high.astype(F32), low.astype(F32)], 0).T.astype(BF16)
    split_out[...] = jnp.concatenate([pair, pair], 1)
    floor, ceiling = levels(tau_ref)
    level_out[0:1, :] = jnp.full((1, 128), floor, F32)
    level_out[1:2, :] = jnp.full((1, 128), ceiling, F32)

    send_gram.wait()
    gram = gram_out[...] + gram_in[...]
    row_bound = jnp.max(jnp.sum(jnp.abs(gram), axis=1, keepdims=True), axis=0, keepdims=True)
    eta = 1.0 / (penalty_fit * row_bound + 12.0 * penalty_tv)

    def pass_on(step, turn, x, coef):
        coefs[step, x + 1] = coef
        for way, block in ((0, coef[:, 0:128]), (1, pltpu.roll(coef[:, 128:256], GZ, 1))):
            edge_out[step, way, x] = packed(block)
            send_y(step, way, x).start()

        @pl.when(turn == 0)
        def _():
            send_x(step, 1).start()

        @pl.when(turn == 1)
        def _():
            send_x(step, 0).start()

    def residual(step, turn, x, coef):
        right = stacked(coef)
        total = None
        for block in range(image.shape[1] // ROWS):
            rows = slice(block * ROWS, (block + 1) * ROWS)
            seen = image[x, rows, :]
            target = seen - product(split_out[rows, :], right)
            if step == 1:
                target = target + dual[x, rows, :]
            new = jnp.clip(target, floor, ceiling)
            if step == 0:
                dual[x, rows, :] = new
            else:
                base_out[x, rows, :] = seen + new
            total = add_up(total, rows, *halves(new))
        number = (step + 1) * PX + turn
        sums[number] = total * mask_of(x)
        give_sum(number)

    def smooth(step, turn, x):
        def left_wall(at):
            rise = coefs[step, at + 1] - coefs[step, at]
            if step == 1:
                rise = rise + w_x[0, at]
            w_x[step, at] = dual_of(rise)

        @pl.when(turn == 0)
        def _():
            send_x(step, 0).wait_recv()
            left_wall(PX - 1)

        @pl.when(turn == 1)
        def _():
            send_x(step, 1).wait_recv()
            left_wall(0)

        send_y(step, 0, x).wait_recv()
        send_y(step, 1, x).wait_recv()
        here = coefs[step, x + 1]
        rise_x = coefs[step, x + 2] - here
        after = unpacked(edge_in[step, 0, x], 128 - GZ)
        before = unpacked(edge_in[step, 1, x], 0)
        turned_y = pltpu.roll(here, LAYER - GZ, 1)
        next_y = jnp.concatenate(
            [turned_y[:, 0:128], jnp.where(short >= 128 - GZ, after, turned_y[:, 128:256])], 1
        )
        rise_y = valid_y * (next_y - here)
        rise_z = valid_z * (pltpu.roll(here, LAYER - 1, 1) - here)
        rise_edge = has_left * (here[:, 0:128] - before)
        if step == 1:
            rise_x = rise_x + w_x[0, x + 1]
            rise_y = rise_y + w_y[x]
            rise_z = rise_z + w_z[x]
            rise_edge = rise_edge + w_edge[x]
        new_x, new_y, new_z, new_edge = (dual_of(rise) for rise in (rise_x, rise_y, rise_z, rise_edge))
        summed = w_x[step, x] - new_x
        turned_y = pltpu.roll(new_y, GZ, 1)
        prev_y = jnp.concatenate(
            [jnp.where(short < GZ, new_edge, turned_y[:, 0:128]), turned_y[:, 128:256]], 1
        )
        summed = summed + (prev_y - new_y)
        summed = summed + (pltpu.roll(new_z, 1, 1) - new_z)
        w_x[step, x + 1] = new_x
        if step == 0:
            w_y[x] = new_y
            w_z[x] = new_z
            w_edge[x] = new_edge
        return summed

    def total_of(number):
        send_sum(number).wait_recv()
        return sums[number] + partner[number]

    def second(turn, carry):
        x = layer_at(turn)
        coef = eta * total_of(turn)
        pass_on(0, turn, x, coef)
        residual(0, turn, x, coef)
        return carry

    def third(turn, carry):
        x = layer_at(turn)
        summed = smooth(0, turn, x)
        change = total_of(PX + turn) - summed
        first_v[x] = change
        coef = coefs[0, x + 1] + eta * (2.0 * change)
        pass_on(1, turn, x, coef)
        residual(1, turn, x, coef)
        return carry

    def last(turn, carry):
        x = layer_at(turn)
        summed = smooth(1, turn, x)
        change = total_of(2 * PX + turn) - summed
        coef_out[x] = coefs[1, x + 1] + eta * (2.0 * change - first_v[x])
        return carry

    lax.fori_loop(0, PX, second, 0)
    lax.fori_loop(0, PX, third, 0)
    lax.fori_loop(0, PX, last, 0)

    for number in range(3 * PX - WINDOW, 3 * PX):
        send_sum(number).wait_send()
    for step in range(2):
        for way in range(2):
            send_x(step, way).wait_send()
            for x in range(PX):
                send_y(step, way, x).wait_send()


def finish(base, coef_ref, split_ref, mask_ref, level_ref, coef_out, residual_out, result, out_sem, coef_sem):
    floor, ceiling = level_ref[0:1, 0:1], level_ref[1:2, 0:1]

    def columns(x):
        return pl.ds(pl.multiple_of(x * LAYER, LAYER), LAYER)

    def put(x):
        return pltpu.make_async_copy(result.at[x], residual_out.at[:, columns(x)], out_sem.at[x])

    def put_coef(x):
        return pltpu.make_async_copy(coef_ref.at[x], coef_out.at[:, columns(x)], coef_sem.at[x])

    for x in range(PX):
        put_coef(x).start()

    def layer(x, carry):
        right = stacked(coef_ref[x])
        mask = mask_ref[:, columns(x)]
        for block in range(result.shape[1] // ROWS):
            rows = slice(block * ROWS, (block + 1) * ROWS)
            target = base[x, rows, :] - product(split_ref[rows, :], right)
            result[x, rows, :] = mask * (target - jnp.clip(target, floor, ceiling))
        put(x).start()
        return carry

    lax.fori_loop(0, PX, layer, 0)
    for x in range(PX):
        put_coef(x).wait()
        put(x).wait()


def per_device(observed, covariates, voxel_mask, tau_index):
    subjects, voxels = observed.shape
    inputs = [
        pltpu.with_memory_space_constraint(value, pltpu.HBM)
        for value in (observed, covariates.T, voxel_mask.reshape(1, voxels))
    ]
    vmem = pl.BlockSpec(memory_space=pltpu.VMEM)
    smem = pl.BlockSpec(memory_space=pltpu.SMEM)
    hbm = pl.BlockSpec(memory_space=pltpu.HBM)
    dma = pltpu.SemaphoreType.DMA
    made = pl.pallas_call(
        iterate,
        out_shape=(
            pltpu.VMEM((PX, subjects, LAYER), F32),
            pltpu.VMEM((PX, COVARS, LAYER), F32),
            pltpu.VMEM((subjects, 4 * COVARS), BF16),
            pltpu.VMEM((1, voxels), F32),
            pltpu.VMEM((2, 128), F32),
        ),
        in_specs=[hbm, hbm, hbm, smem],
        out_specs=(vmem,) * 5,
        scratch_shapes=[
            pltpu.VMEM((PX, subjects, LAYER), F32),
            pltpu.VMEM((PX, subjects, LAYER), F32),
            pltpu.VMEM((3 * PX, COVARS, LAYER), F32),
            pltpu.VMEM((3 * PX, COVARS, LAYER), F32),
            pltpu.VMEM((2, PX + 2, COVARS, LAYER), F32),
            pltpu.VMEM((PX, COVARS, LAYER), F32),
            pltpu.VMEM((2, PX + 1, COVARS, LAYER), F32),
            pltpu.VMEM((PX, COVARS, LAYER), F32),
            pltpu.VMEM((PX, COVARS, LAYER), F32),
            pltpu.VMEM((PX, COVARS, 128), F32),
            pltpu.VMEM((2, 2, PX, COVARS // 4, 128), F32),
            pltpu.VMEM((2, 2, PX, COVARS // 4, 128), F32),
            pltpu.VMEM((COVARS, COVARS), F32),
            pltpu.VMEM((COVARS, COVARS), F32),
            pltpu.VMEM((2 * COVARS, subjects), BF16),
            pltpu.VMEM((COVARS, subjects), F32),
            pltpu.VMEM((1, voxels), jnp.int32),
            dma((PX,)), dma, dma, dma((3 * PX,)), dma((3 * PX,)), dma((2, 2)), dma((2, 2)),
            dma((2, 2, PX)), dma((2, 2, PX)), dma, dma,
        ],
        compiler_params=pltpu.CompilerParams(
            collective_id=0, has_side_effects=True, vmem_limit_bytes=40 << 20
        ),
        name="iterate",
    )(*inputs, tau_index)
    return pl.pallas_call(
        finish,
        out_shape=(
            jax.ShapeDtypeStruct((COVARS, voxels), F32),
            jax.ShapeDtypeStruct((subjects, voxels), F32),
        ),
        in_specs=[vmem] * 5,
        out_specs=(hbm, hbm),
        scratch_shapes=[pltpu.VMEM((PX, subjects, LAYER), F32), dma((PX,)), dma((PX,))],
        compiler_params=pltpu.CompilerParams(vmem_limit_bytes=24 << 20),
        name="finish",
    )(*made)


def solution(mesh):
    return jax.shard_map(
        per_device,
        mesh=mesh,
        in_specs=(P("sub", "vox"), P("sub", None), P("vox"), P()),
        out_specs=(P(None, "vox"), P("sub", "vox")),
        check_vma=False,
    )
```

time: 56 us -> 53 us (0.946); the launches traced: 55.8 us -> 52.1 us
  Pallas kernels: 52.9 us -> 50.8 us
  local copies, waits for them, and re-layouts: 1.64 us -> 0 us
    pallas_call x1, Pallas kernels: 48.9 us -> 46.7 us  [per_device(): pl.pallas_call(iterate, out_shape=(pltpu.VMEM((PX, subjects, LAYER), F32)...]
    unnamed x4 -> x0, local copies, waits for them, and re-layouts: 1.64 us -> none
where the time goes in v1:
time: 53 us; the launch traced here: 52.1 us
  Pallas kernels  50.8 us (96%)
  between operations  1.28 us (2%)
    pallas_call x1, Pallas kernels, per_device(): pl.pallas_call(iterate, out_shape=(pltpu.VMEM((PX, subjects, LAYER), F32)...  46.7 us
    pallas_call x1, Pallas kernels, per_device(): pl.pallas_call(finish, out_shape=(jax.ShapeDtypeStruct((COVARS, voxels),...  4.04 us

profile of v1, /device:TPU:1, one launch (start us, length us, event | category | flops | bytes accessed | tf_op | source)
XLA Modules:
  0.0 52.1 jit_solution(2897045764448617231)
XLA Ops:
  1.3 46.7 %iterate.1 = (f32[8,1024,256]{2,1,0:T(8,128)S(1)}, f32[8,64,256]{2,1,0:T(8,128)S(1)}, bf16[1024,256]{1,0:T(8,128)(2,1)S(1)}, f32[1,2048]{1,0:T(1,128)S(1)}, f32[2,128]{1,0:T(2,128)S(1)}) custom-call(f32[1024,2048]{1,0:T(8,128)} %image_hbm.1, f32[64,1024]{1,0:T(8,128)} %bitcast.2, s32[1,2048]{1,0:T(1,128)} %bitcast.3, s32[1]{0:T(128)S(6)} %copy.6.tau_ref), custom_call_target="tpu_custom_call" | custom-call | tf_op jit(solution)/shard_map/iterate/pallas_call | solution.py:370
  48.0 4.0 %finish.1 = (f32[64,2048]{1,0:T(8,128)}, f32[1024,2048]{1,0:T(8,128)}) custom-call(f32[8,1024,256]{2,1,0:T(8,128)S(1)} %get-tuple-element.7.base, f32[8,64,256]{2,1,0:T(8,128)S(1)} %get-tuple-element.8.coef_ref, bf16[1024,256]{1,0:T(8,128)(2,1)S(1)} %get-tuple-element.9.split_ref, f32[1,2048]{1,0:T(1,128)S(1)} %get-tuple-element.10.mask_ref, ...), custom_call_target="tpu_custom_call" | custom-call | tf_op jit(solution)/shard_map/finish/pallas_call | solution.py:407

commit v2 on v1

--- a/solution.py
+++ b/solution.py
@@ -15,7 +15,7 @@
 QUANT = 20
 LAYER = PY * GZ
 ROWS = 256
-WINDOW = 2
+WINDOW = 4
 
 penalty_fit = 1.0
 penalty_tv = 1.0
@@ -57,7 +57,7 @@
     base_out, coef_out, split_out, mask_out, level_out,
     image, dual, sums, partner, coefs, first_v, w_x, w_y, w_z, w_edge,
     edge_out, edge_in, gram_out, gram_in, covs_t, covs_ref, mask_ref,
-    load_sem, covs_sem, mask_sem, sum_send, sum_recv, x_send, x_recv, y_send, y_recv, gram_send, gram_recv,
+    load_sem, covs_sem, mask_sem, sum_send, sum_recv, x_send, x_recv, y_send, y_recv, gram_send, gram_recv, mate_in, all_in,
 ):
     part = lax.axis_index("sub")
     place = lax.axis_index("vox")
@@ -73,8 +73,13 @@
     pencil_y = lax.rem(lax.rem(place + NPY // 2, pencils), NPY)
 
     barrier = pltpu.get_barrier_semaphore()
-    for device in (mate, right_x, left_x, right_y, behind_y):
-        pl.semaphore_signal(barrier, inc=1, device_id=device, device_id_type=MESH)
+
+    def signal(semaphore, device):
+        pl.semaphore_signal(semaphore, inc=1, device_id=device, device_id_type=MESH)
+
+    @pl.when(part == 0)
+    def _():
+        signal(barrier, mate)
 
     def layer_at(turn):
         return lax.rem(turn + PX - 1, PX)
@@ -125,6 +130,11 @@
     load_mask.start()
     for turn in range(2):
         load(layer_at(turn)).start()
+
+    @pl.when(part == 1)
+    def _():
+        pl.semaphore_wait(barrier, 1)
+        signal(mate_in, mate)
 
     load_covs.wait()
     covs = covs_ref[...]
@@ -174,9 +184,11 @@
             total = add_up(total, rows, *halves(image[x, rows, :]))
         sums[turn] = total * mask_of(x)
 
-        @pl.when(turn == 0)
-        def _():
-            pl.semaphore_wait(barrier, 5)
+        @pl.when((turn == 0) & (part == 0))
+        def _():
+            pl.semaphore_wait(mate_in, 1)
+            for device in (right_x, left_x, right_y, left_y):
+                signal(barrier, device)
 
         give_sum(turn)
 
@@ -312,6 +324,15 @@
         change = total_of(2 * PX + turn) - summed
         coef_out[x] = coefs[1, x + 1] + eta * (2.0 * change - first_v[x])
         return carry
+
+    @pl.when(part == 0)
+    def _():
+        pl.semaphore_wait(barrier, 4)
+        signal(all_in, mate)
+
+    @pl.when(part == 1)
+    def _():
+        pl.semaphore_wait(all_in, 1)
 
     lax.fori_loop(0, PX, second, 0)
     lax.fori_loop(0, PX, third, 0)
@@ -398,6 +419,7 @@
             pltpu.VMEM((1, voxels), jnp.int32),
             dma((PX,)), dma, dma, dma((3 * PX,)), dma((3 * PX,)), dma((2, 2)), dma((2, 2)),
             dma((2, 2, PX)), dma((2, 2, PX)), dma, dma,
+            pltpu.SemaphoreType.REGULAR, pltpu.SemaphoreType.REGULAR,
         ],
         compiler_params=pltpu.CompilerParams(
             collective_id=0, has_side_effects=True, vmem_limit_bytes=40 << 20

time: 53 us -> 49.3 us (0.930); the launches traced: 52.1 us -> 49.1 us
  Pallas kernels: 50.8 us -> 47.9 us
    pallas_call x1, Pallas kernels: 46.7 us -> 43.8 us  [per_device(): pl.pallas_call(iterate, out_shape=(pltpu.VMEM((PX, subjects, LAYER), F32)...]
where the time goes in v2:
time: 49.3 us; the launch traced here: 49.1 us
  Pallas kernels  47.9 us (97%)
  between operations  1.28 us (3%)
    pallas_call x1, Pallas kernels, per_device(): pl.pallas_call(iterate, out_shape=(pltpu.VMEM((PX, subjects, LAYER), F32)...  43.8 us
    pallas_call x1, Pallas kernels, per_device(): pl.pallas_call(finish, out_shape=(jax.ShapeDtypeStruct((COVARS, voxels),...  4.04 us

profile of v2, /device:TPU:1, one launch (start us, length us, event | category | flops | bytes accessed | tf_op | source)
XLA Modules:
  0.0 49.1 jit_solution(15588387550631601203)
XLA Ops:
  1.3 43.8 %iterate.1 = (f32[8,1024,256]{2,1,0:T(8,128)S(1)}, f32[8,64,256]{2,1,0:T(8,128)S(1)}, bf16[1024,256]{1,0:T(8,128)(2,1)S(1)}, f32[1,2048]{1,0:T(1,128)S(1)}, f32[2,128]{1,0:T(2,128)S(1)}) custom-call(f32[1024,2048]{1,0:T(8,128)} %image_hbm.1, f32[64,1024]{1,0:T(8,128)} %bitcast.2, s32[1,2048]{1,0:T(1,128)} %bitcast.3, s32[1]{0:T(128)S(6)} %copy.6.tau_ref), custom_call_target="tpu_custom_call" | custom-call | tf_op jit(solution)/shard_map/iterate/pallas_call | solution.py:391
  45.1 4.0 %finish.1 = (f32[64,2048]{1,0:T(8,128)}, f32[1024,2048]{1,0:T(8,128)}) custom-call(f32[8,1024,256]{2,1,0:T(8,128)S(1)} %get-tuple-element.7.base, f32[8,64,256]{2,1,0:T(8,128)S(1)} %get-tuple-element.8.coef_ref, bf16[1024,256]{1,0:T(8,128)(2,1)S(1)} %get-tuple-element.9.split_ref, f32[1,2048]{1,0:T(1,128)S(1)} %get-tuple-element.10.mask_ref, ...), custom_call_target="tpu_custom_call" | custom-call | tf_op jit(solution)/shard_map/finish/pallas_call | solution.py:429

commit v3 on v2

--- a/solution.py
+++ b/solution.py
@@ -322,7 +322,18 @@
         x = layer_at(turn)
         summed = smooth(1, turn, x)
         change = total_of(2 * PX + turn) - summed
-        coef_out[x] = coefs[1, x + 1] + eta * (2.0 * change - first_v[x])
+        coef = coefs[1, x + 1] + eta * (2.0 * change - first_v[x])
+        coef_out[x] = coef
+
+        @pl.when(turn < PX - 1)
+        def _():
+            right = stacked(coef)
+            mask = mask_of(x)
+            for block in range(image.shape[1] // ROWS):
+                rows = slice(block * ROWS, (block + 1) * ROWS)
+                target = base_out[x, rows, :] - product(split_out[rows, :], right)
+                base_out[x, rows, :] = mask * (target - jnp.clip(target, floor, ceiling))
+
         return carry
 
     @pl.when(part == 0)
@@ -348,34 +359,34 @@
 
 
 def finish(base, coef_ref, split_ref, mask_ref, level_ref, coef_out, residual_out, result, out_sem, coef_sem):
+    subjects = result.shape[0]
+    final = PX - 2
+
+    def columns(x):
+        return pl.ds(x * LAYER, LAYER)
+
+    copies = [
+        pltpu.make_async_copy(base.at[x], residual_out.at[:, columns(x)], out_sem.at[x])
+        for x in range(PX) if x != final
+    ]
+    copies += [
+        pltpu.make_async_copy(coef_ref.at[x], coef_out.at[:, columns(x)], coef_sem.at[x])
+        for x in range(PX)
+    ]
+    for copy in copies:
+        copy.start()
+
     floor, ceiling = level_ref[0:1, 0:1], level_ref[1:2, 0:1]
-
-    def columns(x):
-        return pl.ds(pl.multiple_of(x * LAYER, LAYER), LAYER)
-
-    def put(x):
-        return pltpu.make_async_copy(result.at[x], residual_out.at[:, columns(x)], out_sem.at[x])
-
-    def put_coef(x):
-        return pltpu.make_async_copy(coef_ref.at[x], coef_out.at[:, columns(x)], coef_sem.at[x])
-
-    for x in range(PX):
-        put_coef(x).start()
-
-    def layer(x, carry):
-        right = stacked(coef_ref[x])
-        mask = mask_ref[:, columns(x)]
-        for block in range(result.shape[1] // ROWS):
-            rows = slice(block * ROWS, (block + 1) * ROWS)
-            target = base[x, rows, :] - product(split_ref[rows, :], right)
-            result[x, rows, :] = mask * (target - jnp.clip(target, floor, ceiling))
-        put(x).start()
-        return carry
-
-    lax.fori_loop(0, PX, layer, 0)
-    for x in range(PX):
-        put_coef(x).wait()
-        put(x).wait()
+    right = stacked(coef_ref[final])
+    mask = mask_ref[:, columns(final)]
+    for block in range(subjects // ROWS):
+        rows = slice(block * ROWS, (block + 1) * ROWS)
+        target = base[final, rows, :] - product(split_ref[rows, :], right)
+        result[rows, :] = mask * (target - jnp.clip(target, floor, ceiling))
+    copy = pltpu.make_async_copy(result, residual_out.at[:, columns(final)], out_sem.at[final])
+    copy.start()
+    for copy in (*copies, copy):
+        copy.wait()
 
 
 def per_device(observed, covariates, voxel_mask, tau_index):
@@ -434,7 +445,7 @@
         ),
         in_specs=[vmem] * 5,
         out_specs=(hbm, hbm),
-        scratch_shapes=[pltpu.VMEM((PX, subjects, LAYER), F32), dma((PX,)), dma((PX,))],
+        scratch_shapes=[pltpu.VMEM((subjects, LAYER), F32), dma((PX,)), dma((PX,))],
         compiler_params=pltpu.CompilerParams(vmem_limit_bytes=24 << 20),
         name="finish",
     )(*made)

time: 49.3 us -> 49 us (level)
  no operation moved by 1% of the time
where the time goes in v3:
time: 49 us; the launch traced here: 48.8 us
  Pallas kernels  47.5 us (97%)
  between operations  1.28 us (3%)
    pallas_call x1, Pallas kernels, per_device(): pl.pallas_call(iterate, out_shape=(pltpu.VMEM((PX, subjects, LAYER), F32)...  43.8 us
    pallas_call x1, Pallas kernels, per_device(): pl.pallas_call(finish, out_shape=(jax.ShapeDtypeStruct((COVARS, voxels),...  3.67 us

profile of v3, /device:TPU:1, one launch (start us, length us, event | category | flops | bytes accessed | tf_op | source)
XLA Modules:
  0.0 48.8 jit_solution(16841922846704170186)
XLA Ops:
  1.3 43.8 %iterate.1 = (f32[8,1024,256]{2,1,0:T(8,128)S(1)}, f32[8,64,256]{2,1,0:T(8,128)S(1)}, bf16[1024,256]{1,0:T(8,128)(2,1)S(1)}, f32[1,2048]{1,0:T(1,128)S(1)}, f32[2,128]{1,0:T(2,128)S(1)}) custom-call(f32[1024,2048]{1,0:T(8,128)} %image_hbm.1, f32[64,1024]{1,0:T(8,128)} %bitcast.2, s32[1,2048]{1,0:T(1,128)} %bitcast.3, s32[1]{0:T(128)S(6)} %copy.6.tau_ref), custom_call_target="tpu_custom_call" | custom-call | tf_op jit(solution)/shard_map/iterate/pallas_call | solution.py:402
  45.1 3.7 %finish.1 = (f32[64,2048]{1,0:T(8,128)}, f32[1024,2048]{1,0:T(8,128)}) custom-call(f32[8,1024,256]{2,1,0:T(8,128)S(1)} %get-tuple-element.7.base, f32[8,64,256]{2,1,0:T(8,128)S(1)} %get-tuple-element.8.coef_ref, bf16[1024,256]{1,0:T(8,128)(2,1)S(1)} %get-tuple-element.9.split_ref, f32[1,2048]{1,0:T(1,128)S(1)} %get-tuple-element.10.mask_ref, ...), custom_call_target="tpu_custom_call" | custom-call | tf_op jit(solution)/shard_map/finish/pallas_call | solution.py:440

commit v4 on v3

--- a/solution.py
+++ b/solution.py
@@ -15,7 +15,6 @@
 QUANT = 20
 LAYER = PY * GZ
 ROWS = 256
-WINDOW = 4
 
 penalty_fit = 1.0
 penalty_tv = 1.0
@@ -87,36 +86,40 @@
     def load(x):
         return pltpu.make_async_copy(
             image_hbm.at[:, pl.ds(pl.multiple_of(x * LAYER, LAYER), LAYER)],
-            image.at[x], load_sem.at[x],
+            image.at[x], load_sem.at[lax.rem(x, 2)],
+        )
+
+    def to_mate(source, target, receipt):
+        return pltpu.make_async_remote_copy(
+            src_ref=source, dst_ref=target, send_sem=sum_send, recv_sem=receipt,
+            device_id=mate, device_id_type=MESH,
         )
 
     def send_sum(number):
-        return pltpu.make_async_remote_copy(
-            src_ref=sums.at[number], dst_ref=partner.at[number],
-            send_sem=sum_send.at[number], recv_sem=sum_recv.at[number],
-            device_id=mate, device_id_type=MESH,
-        )
-
-    def give_sum(number):
-        @pl.when(number >= WINDOW)
-        def _():
-            send_sum(number - WINDOW).wait_send()
-
-        send_sum(number).start()
+        slot = lax.rem(number, 2 * PX)
+        return to_mate(sums.at[number], partner.at[number], sum_recv.at[slot])
 
     def send_x(step, way):
         source, target, device = ((1, PX + 1, left_x), (PX, 0, right_x))[way]
         return pltpu.make_async_remote_copy(
             src_ref=coefs.at[step, source], dst_ref=coefs.at[step, target],
-            send_sem=x_send.at[step, way], recv_sem=x_recv.at[step, way],
+            send_sem=x_send, recv_sem=x_recv.at[step, way],
             device_id=device, device_id_type=MESH,
         )
 
-    def send_y(step, way, x):
+    def send_y(step, way, turn):
         return pltpu.make_async_remote_copy(
-            src_ref=edge_out.at[step, way, x], dst_ref=edge_in.at[step, way, x],
-            send_sem=y_send.at[step, way, x], recv_sem=y_recv.at[step, way, x],
+            src_ref=edge_out.at[step, turn, way], dst_ref=edge_in.at[step, turn, way],
+            send_sem=y_send, recv_sem=y_recv.at[step, lax.div(turn, 2)],
             device_id=(left_y, far_y)[way], device_id_type=MESH,
+        )
+
+    def both_y(step, turn):
+        turns = pl.ds(turn, 2)
+        return pltpu.make_async_remote_copy(
+            src_ref=edge_out.at[step, turns], dst_ref=edge_in.at[step, turns],
+            send_sem=y_send, recv_sem=y_recv.at[step, lax.div(turn, 2)],
+            device_id=left_y, device_id_type=MESH,
         )
 
     send_gram = pltpu.make_async_remote_copy(
@@ -190,7 +193,7 @@
             for device in (right_x, left_x, right_y, left_y):
                 signal(barrier, device)
 
-        give_sum(turn)
+        send_sum(turn).start()
 
         @pl.when(turn == 0)
         def _():
@@ -217,8 +220,8 @@
     def pass_on(step, turn, x, coef):
         coefs[step, x + 1] = coef
         for way, block in ((0, coef[:, 0:128]), (1, pltpu.roll(coef[:, 128:256], GZ, 1))):
-            edge_out[step, way, x] = packed(block)
-            send_y(step, way, x).start()
+            edge_out[step, turn, way] = packed(block)
+            send_y(step, way, turn).start()
 
         @pl.when(turn == 0)
         def _():
@@ -245,7 +248,7 @@
             total = add_up(total, rows, *halves(new))
         number = (step + 1) * PX + turn
         sums[number] = total * mask_of(x)
-        give_sum(number)
+        send_sum(number).start()
 
     def smooth(step, turn, x):
         def left_wall(at):
@@ -264,12 +267,14 @@
             send_x(step, 1).wait_recv()
             left_wall(0)
 
-        send_y(step, 0, x).wait_recv()
-        send_y(step, 1, x).wait_recv()
+        @pl.when(lax.rem(turn, 2) == 0)
+        def _():
+            both_y(step, turn).wait_recv()
+
         here = coefs[step, x + 1]
         rise_x = coefs[step, x + 2] - here
-        after = unpacked(edge_in[step, 0, x], 128 - GZ)
-        before = unpacked(edge_in[step, 1, x], 0)
+        after = unpacked(edge_in[step, turn, 0], 128 - GZ)
+        before = unpacked(edge_in[step, turn, 1], 0)
         turned_y = pltpu.roll(here, LAYER - GZ, 1)
         next_y = jnp.concatenate(
             [turned_y[:, 0:128], jnp.where(short >= 128 - GZ, after, turned_y[:, 128:256])], 1
@@ -349,13 +354,15 @@
     lax.fori_loop(0, PX, third, 0)
     lax.fori_loop(0, PX, last, 0)
 
-    for number in range(3 * PX - WINDOW, 3 * PX):
-        send_sum(number).wait_send()
-    for step in range(2):
-        for way in range(2):
-            send_x(step, way).wait_send()
-            for x in range(PX):
-                send_y(step, way, x).wait_send()
+    to_mate(sums, partner, sum_recv.at[0]).wait_send()
+    pltpu.make_async_remote_copy(
+        src_ref=coefs.at[:, pl.ds(1, 2)], dst_ref=coefs.at[:, pl.ds(1, 2)], send_sem=x_send, recv_sem=x_recv.at[0, 0],
+        device_id=left_x, device_id_type=MESH,
+    ).wait_send()
+    pltpu.make_async_remote_copy(
+        src_ref=edge_out, dst_ref=edge_in, send_sem=y_send, recv_sem=y_recv.at[0, 0],
+        device_id=left_y, device_id_type=MESH,
+    ).wait_send()
 
 
 def finish(base, coef_ref, split_ref, mask_ref, level_ref, coef_out, residual_out, result, out_sem, coef_sem):
@@ -366,11 +373,11 @@
         return pl.ds(x * LAYER, LAYER)
 
     copies = [
-        pltpu.make_async_copy(base.at[x], residual_out.at[:, columns(x)], out_sem.at[x])
+        pltpu.make_async_copy(base.at[x], residual_out.at[:, columns(x)], out_sem)
         for x in range(PX) if x != final
     ]
     copies += [
-        pltpu.make_async_copy(coef_ref.at[x], coef_out.at[:, columns(x)], coef_sem.at[x])
+        pltpu.make_async_copy(coef_ref.at[x], coef_out.at[:, columns(x)], coef_sem)
         for x in range(PX)
     ]
     for copy in copies:
@@ -383,10 +390,9 @@
         rows = slice(block * ROWS, (block + 1) * ROWS)
         target = base[final, rows, :] - product(split_ref[rows, :], right)
         result[rows, :] = mask * (target - jnp.clip(target, floor, ceiling))
-    copy = pltpu.make_async_copy(result, residual_out.at[:, columns(final)], out_sem.at[final])
-    copy.start()
-    for copy in (*copies, copy):
-        copy.wait()
+    pltpu.make_async_copy(result, residual_out.at[:, columns(final)], out_sem).start()
+    pltpu.make_async_copy(coef_ref, coef_ref, coef_sem).wait()
+    pltpu.make_async_copy(base, base, out_sem).wait()
 
 
 def per_device(observed, covariates, voxel_mask, tau_index):
@@ -421,15 +427,15 @@
             pltpu.VMEM((PX, COVARS, LAYER), F32),
             pltpu.VMEM((PX, COVARS, LAYER), F32),
             pltpu.VMEM((PX, COVARS, 128), F32),
-            pltpu.VMEM((2, 2, PX, COVARS // 4, 128), F32),
-            pltpu.VMEM((2, 2, PX, COVARS // 4, 128), F32),
+            pltpu.VMEM((2, PX, 2, COVARS // 4, 128), F32),
+            pltpu.VMEM((2, PX, 2, COVARS // 4, 128), F32),
             pltpu.VMEM((COVARS, COVARS), F32),
             pltpu.VMEM((COVARS, COVARS), F32),
             pltpu.VMEM((2 * COVARS, subjects), BF16),
             pltpu.VMEM((COVARS, subjects), F32),
             pltpu.VMEM((1, voxels), jnp.int32),
-            dma((PX,)), dma, dma, dma((3 * PX,)), dma((3 * PX,)), dma((2, 2)), dma((2, 2)),
-            dma((2, 2, PX)), dma((2, 2, PX)), dma, dma,
+            dma((2,)), dma, dma, dma, dma((2 * PX,)), dma, dma((2, 2)),
+            dma, dma((2, PX // 2)), dma, dma,
             pltpu.SemaphoreType.REGULAR, pltpu.SemaphoreType.REGULAR,
         ],
         compiler_params=pltpu.CompilerParams(
@@ -445,7 +451,7 @@
         ),
         in_specs=[vmem] * 5,
         out_specs=(hbm, hbm),
-        scratch_shapes=[pltpu.VMEM((subjects, LAYER), F32), dma((PX,)), dma((PX,))],
+        scratch_shapes=[pltpu.VMEM((subjects, LAYER), F32), dma, dma],
         compiler_params=pltpu.CompilerParams(vmem_limit_bytes=24 << 20),
         name="finish",
     )(*made)

time: 49 us -> 48.1 us (0.982)
  Pallas kernels: 47.5 us -> 46.6 us
    pallas_call x1, Pallas kernels: 43.8 us -> 43.1 us  [per_device(): pl.pallas_call(iterate, out_shape=(pltpu.VMEM((PX, subjects, LAYER), F32)...]
where the time goes in v4:
time: 48.1 us; the launch traced here: 47.9 us
  Pallas kernels  46.6 us (97%)
  between operations  1.28 us (3%)
    pallas_call x1, Pallas kernels, per_device(): pl.pallas_call(iterate, out_shape=(pltpu.VMEM((PX, subjects, LAYER), F32)...  43.1 us
    pallas_call x1, Pallas kernels, per_device(): pl.pallas_call(finish, out_shape=(jax.ShapeDtypeStruct((COVARS, voxels),...  3.55 us

profile of v4, /device:TPU:1, one launch (start us, length us, event | category | flops | bytes accessed | tf_op | source)
XLA Modules:
  0.0 47.9 jit_solution(11191380129437407738)
XLA Ops:
  1.3 43.1 %iterate.1 = (f32[8,1024,256]{2,1,0:T(8,128)S(1)}, f32[8,64,256]{2,1,0:T(8,128)S(1)}, bf16[1024,256]{1,0:T(8,128)(2,1)S(1)}, f32[1,2048]{1,0:T(1,128)S(1)}, f32[2,128]{1,0:T(2,128)S(1)}) custom-call(f32[1024,2048]{1,0:T(8,128)} %image_hbm.1, f32[64,1024]{1,0:T(8,128)} %bitcast.2, s32[1,2048]{1,0:T(1,128)} %bitcast.3, s32[1]{0:T(128)S(6)} %copy.6.tau_ref), custom_call_target="tpu_custom_call" | custom-call | tf_op jit(solution)/shard_map/iterate/pallas_call | solution.py:408
  44.4 3.5 %finish.1 = (f32[64,2048]{1,0:T(8,128)}, f32[1024,2048]{1,0:T(8,128)}) custom-call(f32[8,1024,256]{2,1,0:T(8,128)S(1)} %get-tuple-element.7.base, f32[8,64,256]{2,1,0:T(8,128)S(1)} %get-tuple-element.8.coef_ref, bf16[1024,256]{1,0:T(8,128)(2,1)S(1)} %get-tuple-element.9.split_ref, f32[1,2048]{1,0:T(1,128)S(1)} %get-tuple-element.10.mask_ref, ...), custom_call_target="tpu_custom_call" | custom-call | tf_op jit(solution)/shard_map/finish/pallas_call | solution.py:446
